TPU v7x, 256 devices: a whole 4x4x8 slice. The times are simulated.
256 devices in a mesh: batch: 32 (over x, z), node: 4 (over y), replica: 2 (over core).
Axes of the slice: x: 4, y: 4, z: 8, core: 2. Of those that a mesh axis runs over, the one named last changes fastest.
Arguments:
- embed_table: bfloat16 [32768, 1024], P('batch'), may hold values from -6 to 6
- owner_shard: int32 [64, 256, 1], P(('batch', 'replica')), may hold values from 0 to 31; in each aligned block of 256 rows (0 to 255, 256 to 511, ..., all dimensions but the last counted through in order) at most 12 rows name the same one
- local_row: int32 [64, 256], P(('batch', 'replica')), may hold values from 0 to 1023
- lengths: int32 [64], P(('batch', 'replica')), may hold values from 64 to 256
- spd_bucket: int32 [64, 256, 256], P(('batch', 'replica')), may hold values from 0 to 15, as said below
- degree_bucket: int32 [64, 256], P(('batch', 'replica')), may hold values from 0 to 31, as said below
- w_query: bfloat16 [1024, 1024], P(None, 'node'), may hold values from -0.1875 to 0.1875
- w_key: bfloat16 [1024, 1024], P(None, 'node'), may hold values from -0.1875 to 0.1875
- w_value: bfloat16 [1024, 1024], P(None, 'node'), may hold values from -0.1875 to 0.1875
- w_out: bfloat16 [1024, 1024], P('node'), may hold values from -0.1875 to 0.1875
- spd_bias: float32 [16, 16], P(None, 'node'), may hold values from -4 to 4
- degree_bias: float32 [32, 16], P(None, 'node'), may hold values from -2 to 253
- cotangent: bfloat16 [64, 256, 1024], P(('batch', 'replica')), may hold values from -6 to 6
Outputs:
- table_grad: float32 [32768, 1024], P('batch', ('node', 'replica'))
- query_grad: float32 [1024, 1024], P(None, 'node')
- key_grad: float32 [1024, 1024], P(None, 'node')
- value_grad: float32 [1024, 1024], P(None, 'node')
- out_grad: float32 [1024, 1024], P('node')
- spd_grad: float32 [16, 16], P(None, 'node')
- degree_grad: float32 [32, 16], P(None, 'node')
Inputs may be any that keep to these rules, and one draw needn't show every extreme that they name: `owner_shard`: in each aligned block of 256 slots (the subgraphs of one index of batch and replica) no owner shard is named by more than 12 slots, a bound that some block reaches. `lengths`: slots at or past a subgraph's length are padding. `spd_bucket`: symmetric in its last two dimensions, 0 exactly on the diagonal. `degree_bucket`: some subgraphs hold only buckets below half of 32.
All inputs are finite; a program needn't handle non-finite values.
Results may differ from a plain program's by a relative error of at most 0.015.
Values may be sent and summed in bfloat16 or wider, within the bound.
A program may use at most 64 MiB of HBM per device.

v0:
```python
import jax
import jax.numpy as jnp
from jax import lax
from jax.sharding import PartitionSpec as P

HEAD_DIM = 64
NSPD = 16
NDEG = 32
EPS = 1e-05


def normalize(rows_in):
    widened = rows_in.astype(jnp.float32)
    mean_val = jnp.mean(widened, axis=-1, keepdims=True)
    centred = widened - mean_val
    inv_std = lax.rsqrt(jnp.mean(centred * centred, axis=-1, keepdims=True) + EPS)
    return (centred * inv_std, inv_std)


def on_device(
    embed_table,
    owner_shard,
    local_row,
    lengths,
    spd_bucket,
    degree_bucket,
    w_query,
    w_key,
    w_value,
    w_out,
    spd_bias,
    degree_bias,
    cotangent,
):
    group_count, slot_count, feature_dim = cotangent.shape
    slot_total = group_count * slot_count
    row_count = embed_table.shape[0]
    peer_count = lax.axis_size("batch")
    capacity = 3 * slot_total // (2 * peer_count)
    dest_shard = owner_shard.reshape(slot_total)
    wanted = local_row.reshape(slot_total)
    bucket_hits = (dest_shard[:, None] == jnp.arange(peer_count, dtype=jnp.int32)[None, :]).astype(
        jnp.int32
    )
    bucket_rank = jnp.sum((jnp.cumsum(bucket_hits, axis=0) - bucket_hits) * bucket_hits, axis=1)
    slot_place = dest_shard * capacity + bucket_rank
    requests = jnp.full((peer_count * capacity,), -1, jnp.int32).at[slot_place].set(wanted)
    asked_rows = lax.all_to_all(
        requests.reshape(peer_count, capacity), "batch", split_axis=0, concat_axis=0, tiled=True
    ).reshape(peer_count * capacity)
    present = asked_rows >= 0
    safe_rows = jnp.where(present, asked_rows, 0)
    target_rows = jnp.where(present, asked_rows, row_count)
    fetched = lax.all_to_all(
        embed_table[safe_rows].reshape(peer_count, capacity, feature_dim),
        "batch",
        split_axis=0,
        concat_axis=0,
        tiled=True,
    )
    slot_rows = fetched.reshape(peer_count * capacity, feature_dim)[slot_place]
    x_hat, inv_std = normalize(slot_rows)
    normed = x_hat.astype(jnp.bfloat16)
    local_width = w_query.shape[1]
    head_local = local_width // HEAD_DIM
    head_shape = (group_count, slot_count, head_local, HEAD_DIM)
    score_scale = HEAD_DIM ** (-0.5)

    def project(weight):
        return jnp.dot(normed, weight, preferred_element_type=jnp.float32).astype(jnp.bfloat16)

    queries = project(w_query).reshape(head_shape)
    key_rows = project(w_key).reshape(head_shape)
    values = project(w_value).reshape(head_shape)
    valid_slot = jnp.arange(slot_count, dtype=jnp.int32)[None, :] < lengths[:, None]
    spd_hot = (spd_bucket[..., None] == jnp.arange(NSPD, dtype=jnp.int32)).astype(jnp.float32)
    degree_hot = (degree_bucket[..., None] == jnp.arange(NDEG, dtype=jnp.int32)).astype(jnp.float32)
    spd_term = jnp.einsum("gijb,bh->ghij", spd_hot, spd_bias, precision=lax.Precision.HIGHEST)
    degree_term = jnp.einsum(
        "gjb,bh->ghj", degree_hot, degree_bias, precision=lax.Precision.HIGHEST
    )[:, :, None, :]
    scores = (
        jnp.einsum("gihd,gjhd->ghij", queries, key_rows, preferred_element_type=jnp.float32)
        * score_scale
        + spd_term
        + degree_term
    )
    scores = jnp.where(valid_slot[:, None, None, :], scores, -jnp.inf)
    row_top = jnp.max(scores, axis=-1, keepdims=True)
    exp_scores = jnp.exp(scores - row_top)
    probs = exp_scores / jnp.sum(exp_scores, axis=-1, keepdims=True)
    probs_b = probs.astype(jnp.bfloat16)
    attended = (
        jnp.einsum("ghij,gjhd->gihd", probs_b, values, preferred_element_type=jnp.float32)
        .astype(jnp.bfloat16)
        .reshape(slot_total, local_width)
    )
    d_masked = jnp.where(valid_slot[:, :, None], cotangent, jnp.zeros_like(cotangent)).reshape(
        slot_total, feature_dim
    )
    d_att = jnp.dot(d_masked, w_out.T, preferred_element_type=jnp.float32).astype(jnp.bfloat16)
    out_part = jnp.dot(attended.T, d_masked, preferred_element_type=jnp.float32)
    d_att_h = d_att.reshape(head_shape)
    d_values = (
        jnp.einsum("ghij,gihd->gjhd", probs_b, d_att_h, preferred_element_type=jnp.float32)
        .astype(jnp.bfloat16)
        .reshape(slot_total, local_width)
    )
    d_probs = jnp.einsum("gihd,gjhd->ghij", d_att_h, values, preferred_element_type=jnp.float32)
    d_scores = probs * (d_probs - jnp.sum(probs * d_probs, axis=-1, keepdims=True))
    spd_part = jnp.einsum("gijb,ghij->bh", spd_hot, d_scores, precision=lax.Precision.HIGHEST)
    degree_part = jnp.einsum("gjb,ghij->bh", degree_hot, d_scores, precision=lax.Precision.HIGHEST)
    d_scores_b = d_scores.astype(jnp.bfloat16)
    d_queries = (
        (
            jnp.einsum("ghij,gjhd->gihd", d_scores_b, key_rows, preferred_element_type=jnp.float32)
            * score_scale
        )
        .astype(jnp.bfloat16)
        .reshape(slot_total, local_width)
    )
    d_keys = (
        (
            jnp.einsum("ghij,gihd->gjhd", d_scores_b, queries, preferred_element_type=jnp.float32)
            * score_scale
        )
        .astype(jnp.bfloat16)
        .reshape(slot_total, local_width)
    )
    query_part = jnp.dot(normed.T, d_queries, preferred_element_type=jnp.float32)
    key_part = jnp.dot(normed.T, d_keys, preferred_element_type=jnp.float32)
    value_part = jnp.dot(normed.T, d_values, preferred_element_type=jnp.float32)
    d_normed = (
        jnp.dot(d_queries, w_query.T, preferred_element_type=jnp.float32)
        + jnp.dot(d_keys, w_key.T, preferred_element_type=jnp.float32)
        + jnp.dot(d_values, w_value.T, preferred_element_type=jnp.float32)
    )
    lead_flag = (lax.axis_index("node") == 0).astype(jnp.float32)
    d_rows = lead_flag * d_masked.astype(jnp.float32) + inv_std * (
        d_normed
        - jnp.mean(d_normed, axis=-1, keepdims=True)
        - x_hat * jnp.mean(d_normed * x_hat, axis=-1, keepdims=True)
    )
    send_back = (
        jnp.zeros((peer_count * capacity, feature_dim), jnp.float32).at[slot_place].set(d_rows)
    )
    returned = (
        lax.all_to_all(
            send_back.reshape(peer_count, capacity, feature_dim).astype(jnp.bfloat16),
            "batch",
            split_axis=0,
            concat_axis=0,
            tiled=True,
        )
        .astype(jnp.float32)
        .reshape(peer_count * capacity, feature_dim)
    )
    accum = (
        jnp.zeros((row_count, feature_dim), jnp.float32).at[target_rows].add(returned, mode="drop")
    )
    table_grad = lax.psum_scatter(
        accum.astype(jnp.bfloat16), ("node", "replica"), scatter_dimension=1, tiled=True
    ).astype(jnp.float32)
    summed = lax.psum(
        (query_part, key_part, value_part, out_part, spd_part, degree_part), ("batch", "replica")
    )
    copies = float(peer_count * lax.axis_size("replica"))
    return (
        table_grad,
        summed[0] / copies,
        summed[1] / copies,
        summed[2] / copies,
        summed[3] / copies,
        summed[4] / copies,
        summed[5] / copies,
    )


def solution(mesh):
    placed = (
        P("batch", None),
        P(("batch", "replica"), None, None),
        P(("batch", "replica"), None),
        P(("batch", "replica")),
        P(("batch", "replica"), None, None),
        P(("batch", "replica"), None),
        P(None, "node"),
        P(None, "node"),
        P(None, "node"),
        P("node", None),
        P(None, "node"),
        P(None, "node"),
        P(("batch", "replica"), None, None),
    )
    return jax.shard_map(
        on_device,
        mesh=mesh,
        in_specs=placed,
        out_specs=(
            P("batch", ("node", "replica")),
            P(None, "node"),
            P(None, "node"),
            P(None, "node"),
            P("node", None),
            P(None, "node"),
            P(None, "node"),
        ),
        check_vma=False,
    )
```

profile of v0, /device:TPU:8, one launch (start us, length us, event | category | flops | bytes accessed | tf_op | source)
XLA Modules:
  0.0 310.1 jit_solution(10417535351380792851)
XLA Ops:
  8.0 0.8 fusion.50
  8.8 0.6 reduce-window.6
  9.4 0.2 slice_reduce_fusion
  9.7 0.8 fusion.49
  10.4 0.7 compare_select_fusion.4
  11.1 1.6 scatter_custom_fusion
  12.8 20.9 %all_to_all.19 = s32[32,1,12]{2,1,0:T(1,128)S(1)} all-to-all(s32[32,1,12]{2,1,0:T(1,128)S(1)} %bitcast.120), channel_id=1, replica_groups=mesh['batch'=32,'node'=4,'replica'=2] {'batch'}, dimensions={0} | all-to-all | bytes 3072 | tf_op jit(solution)/shard_map/all_to_all | solution.py:48
  33.7 0.5 broadcast.245
  34.2 0.7 reduce.17
  34.9 0.1 reshape.325
  35.0 0.6 fusion.53
  35.6 2.1 gather_fusion
  37.7 1.1 reshape.327
  38.9 4.7 %all-to-all-start.1 = ((bf16[32,12,1024]{2,1,0:T(8,128)(2,1)}), bf16[32,12,1024]{2,1,0:T(8,128)(2,1)}, u32[]{:S(2)}, u32[]{:S(2)}) async-start(bf16[32,12,1024]{2,1,0:T(8,128)(2,1)} %reshape.327), calls=%async_computation.1 | async-start | bytes 2097152 | tf_op jit(solution)/shard_map/all_to_all | solution.py:54
  43.6 1.3 fusion.2
  44.9 1.4 copy.39
  47.0 0.2 convolution_bitcast_fusion
  47.2 2.3 convolution_convert_fusion.3
  49.5 21.5 %all-to-all-done.1 = bf16[32,12,1024]{2,1,0:T(8,128)(2,1)} async-done(((bf16[32,12,1024]{2,1,0:T(8,128)(2,1)}), bf16[32,12,1024]{2,1,0:T(8,128)(2,1)}, u32[]{:S(2)}, u32[]{:S(2)}) %all-to-all-start.1) | async-done | bytes 786464 | tf_op jit(solution)/shard_map/all_to_all | solution.py:54
  71.1 1.3 reshape.328
  72.4 1.2 gather_fusion.1
  73.6 0.1 convert_reduce_fusion
  73.7 0.3 fusion.26
  74.0 1.5 convolution_convert_fusion.5
  75.5 0.5 convolution_convert_fusion.4
  76.0 0.4 fusion.11
  76.4 0.8 fusion.67
  77.2 0.5 convolution_convert_fusion.2
  77.7 0.4 multiply_reduce_fusion
  78.1 0.2 fusion.66
  78.3 0.2 fusion.17
  78.5 0.8 copy-done.1
  79.3 0.3 fusion.18
  79.5 1.9 convolution_convert_fusion.1
  81.5 2.4 fusion.68
  83.9 1.4 fusion.60
  85.3 1.9 convolution_convert_fusion
  87.3 1.5 fusion.58
  88.7 1.5 fusion.56
  90.2 1.4 fusion.31
  91.6 0.2 reduce-scatter.4.cloned.1.call-start
  91.8 1.8 convolution_add_fusion.1
  93.6 1.4 fusion.65
  95.0 3.8 %scatter_custom_fusion.1 = f32[384,1024]{1,0:T(8,128)} fusion(s32[256]{0:T(256)} %bitcast.125, bf16[256,1024]{1,0:T(8,128)(2,1)S(1)} %gather_fusion.1, f32[256,1024]{1,0:T(8,128)} %get-tuple-element.23, f32[]{:T(128)} %constant.15.clone.1, f32[256]{0:T(256)S(1)} %get-tuple-element.24, f32[256]{0:T(256)S(1)} %get-tuple-element.25, ...), kind=kCustom, calls=%fused_computation.44 | custom fusion | flops 2883584 | bytes 3674884 | tf_op jit(solution)/shard_map/scatter | solution.py:145
  98.8 2.5 convert_element_type.111
  101.3 1.2 convert_element_type.112
  102.5 35.3 %all_to_all.20 = bf16[32,12,1024]{2,1,0:T(8,128)(2,1)} all-to-all(bf16[32,12,1024]{2,1,0:T(8,128)(2,1)S(1)} %convert_element_type.112), channel_id=1, replica_groups=mesh['batch'=32,'node'=4,'replica'=2] {'batch'}, dimensions={0} | all-to-all | bytes 1572864 | tf_op jit(solution)/shard_map/all_to_all | solution.py:148
  137.9 2.4 reshape.377
  140.2 6.6 %scatter_custom_fusion.2 = f32[1024,1024]{1,0:T(8,128)} fusion(s32[384]{0:T(512)} %get-tuple-element.10, f32[384,1024]{1,0:T(8,128)} %reshape.377, f32[]{:T(128)} %constant.15.clone.1), kind=kCustom, calls=%fused_computation.11 | custom fusion | flops 393216 | bytes 4194816 | tf_op jit(solution)/shard_map/scatter-add | solution.py:159
  146.9 3.9 %convert_element_type.113 = bf16[1024,1024]{1,0:T(8,128)(2,1)} convert(f32[1024,1024]{1,0:T(8,128)} %scatter_custom_fusion.2) | non-fusion elementwise | flops 1048576 | bytes 6291456 | tf_op jit(solution)/shard_map/convert_element_type | solution.py:162
  150.8 4.0 %copy.52 = bf16[1024,1024]{0,1:T(8,128)(2,1)} copy(bf16[1024,1024]{1,0:T(8,128)(2,1)} %convert_element_type.113) | data formatting | bytes 4194304
  154.8 1.2 copy-done.2
  156.0 1.3 copy.46
  157.3 4.0 %fusion.19 = f32[16,4]{0,1:T(4,128)S(1)} fusion(f32[4,256,256]{2,0,1:T(4,128)} %copy.46, s32[256,256]{1,0:T(8,128)S(1)} %bitcast.117), kind=kOutput, calls=%fused_computation.39 | convolution fusion | flops 51380224 | bytes 1310976 | tf_op jit(solution)/shard_map/gijb,ghij->bh/dot_general | solution.py:111
  161.2 0.2 fusion.44
  161.5 127.4 %all-reduce = (f32[16,4]{0,1:T(4,128)S(1)}, f32[32,4]{0,1:T(4,128)S(1)}) all-reduce(f32[16,4]{0,1:T(4,128)S(1)} %fusion.19, f32[32,4]{0,1:T(4,128)S(1)} %fusion.44), channel_id=1, replica_groups=mesh['batch'=32,'node'=4,'replica'=2] {'batch','replica'}, use_global_device_ids=true, to_apply=%region_18.19 | all-reduce | flops 192 | bytes 1536 | tf_op jit(solution)/shard_map/psum | solution.py:164
  288.9 0.6 broadcast_multiply_fusion.5
  289.5 0.6 broadcast_multiply_fusion.4
  290.0 5.7 %all-reduce.4.cloned.1.call-done = (f32[1024,256]{1,0:T(8,128)}, f32[1024,256]{1,0:T(8,128)}, f32[1024,256]{1,0:T(8,128)}, f32[256,1024]{1,0:T(8,128)}) async-done(((f32[1024,256]{1,0:T(8,128)}, f32[1024,256]{1,0:T(8,128)}, f32[1024,256]{1,0:T(8,128)}, f32[256,1024]{1,0:T(8,128)}), (f32[1024,256]{1,0:T(8,128)}, f32[1024,256]{1,0:T(8,128)}, f32[1024,256]{1,0:T(8,128)}, ...) | async-done | bytes 4194320 | tf_op jit(solution)/shard_map/psum | solution.py:164
  295.7 2.4 broadcast_multiply_fusion.3
  298.1 1.1 broadcast_multiply_fusion
  299.2 1.5 broadcast_multiply_fusion.1
  300.7 1.1 copy.53
  301.8 0.8 convert_element_type.114
  (51 shorter events, 0.4 us)
Async XLA Ops:
  8.0 27.6 %copy-start = (bf16[1024,1024]{1,0:T(8,128)(2,1)S(1)}, bf16[1024,1024]{1,0:T(8,128)(2,1)}, u32[]{:S(2)}) copy-start(bf16[1024,1024]{1,0:T(8,128)(2,1)} %param.13) | copy-start | bytes 6291460
  11.1 35.8 %copy-start.14 = (s32[256,1]{0,1:T(1,128)}, s32[256,1]{0,1:T(1,128)S(1)}, u32[]{:S(2)}) copy-start(s32[256,1]{0,1:T(1,128)S(1)} %compare_select_fusion.4) | copy-start | bytes 3076
  37.7 5.9 %copy-start.12 = (s32[1,256,256]{2,1,0:T(8,128)S(1)}, s32[1,256,256]{2,1,0:T(8,128)}, u32[]{:S(2)}) copy-start(s32[1,256,256]{2,1,0:T(8,128)} %param.17) | copy-start | bytes 786436
  37.7 5.9 %copy-start.15 = (f32[16,4]{0,1:T(4,128)S(1)}, f32[16,4]{0,1:T(4,128)}, u32[]{:S(2)}) copy-start(f32[16,4]{0,1:T(4,128)} %param.23) | copy-start | bytes 772
  38.9 32.2 %all-to-all-start.1 = ((bf16[32,12,1024]{2,1,0:T(8,128)(2,1)}), bf16[32,12,1024]{2,1,0:T(8,128)(2,1)}, u32[]{:S(2)}, u32[]{:S(2)}) async-start(bf16[32,12,1024]{2,1,0:T(8,128)(2,1)} %reshape.327), calls=%async_computation.1 | async-start | bytes 2097152 | tf_op jit(solution)/shard_map/all_to_all | solution.py:54
  43.5 3.4 %copy-start.16 = (f32[32,4]{0,1:T(4,128)S(1)}, f32[32,4]{0,1:T(4,128)}, u32[]{:S(2)}) copy-start(f32[32,4]{0,1:T(4,128)} %param.24) | copy-start | bytes 1540
  43.5 3.4 %copy-start.17 = (s32[1,256]{1,0:T(1,128)S(1)}, s32[1,256]{1,0:T(1,128)}, u32[]{:S(2)}) copy-start(s32[1,256]{1,0:T(1,128)} %param.18) | copy-start | bytes 3076
  43.5 252.2 %all-reduce.4.cloned.1.call-start = ((), (), s32[]{:S(2)}) async-start(), calls=%async_computation.5 | async-start | bytes 8388608 | tf_op jit(solution)/shard_map/psum | solution.py:164
  73.6 2.0 copy-start.11
  73.6 2.4 copy-start.3
  76.0 1.2 copy-start.9
  76.4 1.6 copy-start.4
  76.4 1.3 copy-start.19
  78.3 1.0 copy-start.1
  87.3 2.9 copy-start.5
  91.6 209.1 %reduce-scatter.4.cloned.1.call-start = ((), (), s32[]{:S(2)}) async-start(), calls=%async_computation.4 | async-start | bytes 2359296
  91.8 1.8 copy-start.10
  154.7 1.2 copy-start.2
  154.7 2.5 copy-start.13
  156.0 5.3 %copy-start.18 = (s32[1,256]{1,0:T(1,128)S(1)}, s32[1,256]{1,0:T(1,128)}, u32[]{:S(2)}) copy-start(s32[1,256]{1,0:T(1,128)} %param.18) | copy-start | bytes 3076
  295.7 2.4 copy-start.6
  295.7 3.5 %copy-start.7 = (f32[1024,256]{1,0:T(8,128)S(1)}, f32[1024,256]{1,0:T(8,128)}, u32[]{:S(2)}) copy-start(f32[1024,256]{1,0:T(8,128)} %get-tuple-element.14) | copy-start | bytes 3145732
  295.7 3.5 %copy-start.8 = (f32[1024,256]{1,0:T(8,128)S(1)}, f32[1024,256]{1,0:T(8,128)}, u32[]{:S(2)}) copy-start(f32[1024,256]{1,0:T(8,128)} %get-tuple-element.15) | copy-start | bytes 3145732
Sparse Core Ops, SparseCore 0:
  91.7 203.9 all-reduce.3
Sparse Core Ops, SparseCore 1:
  154.8 32.6 reduce-scatter.3
where the time goes:
time: 311 us; the launch traced here: 310 us
  blocking collectives  184 us (59%)
  other arithmetic  29.4 us (9%)
  waiting for transfers between devices  27.2 us (9%)
  matrix products  26.8 us (9%)
  local copies, waits for them, and re-layouts  21.6 us (7%)
  between operations  16.5 us (5%)
  starting transfers between devices  4.93 us (2%)
    psum x1, blocking collectives, on_device(): lax.psum((query_part, key_part, value_part, out_part, spd_part, degree_pa...  127 us
    all_to_all x1, blocking collectives, on_device(): lax.all_to_all(send_back.reshape(peer_count, capacity, feature_dim).astyp...  35.3 us
    all_to_all x1, waiting for transfers between devices, on_device(): lax.all_to_all(embed_table[safe_rows].reshape(peer_count, capacity, featu...  21.5 us
    all_to_all x1, blocking collectives, on_device(): lax.all_to_all(requests.reshape(peer_count, capacity), 'batch', split_axi...  20.9 us
    unnamed x42, local copies, waits for them, and re-layouts  7.15 us
    scatter-add x1, other arithmetic, on_device(): jnp.zeros((row_count, feature_dim), jnp.float32).at[target_rows]  6.64 us
  transfers between devices with their start and end apart: 3, of which 2 were waited for; matrix products, arithmetic and copies ran while one was open for 14% of the time, Pallas kernels for 0%

commit v1 on v0

--- a/solution.py
+++ b/solution.py
@@ -162,7 +162,8 @@
         accum.astype(jnp.bfloat16), ("node", "replica"), scatter_dimension=1, tiled=True
     ).astype(jnp.float32)
     summed = lax.psum(
-        (query_part, key_part, value_part, out_part, spd_part, degree_part), ("batch", "replica")
+        lax.psum((query_part, key_part, value_part, out_part, spd_part, degree_part), "batch"),
+        "replica",
     )
     copies = float(peer_count * lax.axis_size("replica"))
     return (

time: 311 us -> 372 us (1.20)
  waiting for transfers between devices: 27.2 us -> 131 us
  blocking collectives: 184 us -> 139 us
    psum x1, waiting for transfers between devices: 5.65 us -> 110 us  [on_device(): lax.psum((query_part, key_part, value_part, out_part, spd_part, degree_pa...]
    psum x1, blocking collectives: 127 us -> 72.5 us  [on_device(): lax.psum((query_part, key_part, value_part, out_part, spd_part, degree_pa...]
    all_to_all x1, blocking collectives: 35.3 us -> 43.3 us  [on_device(): lax.all_to_all(send_back.reshape(peer_count, capacity, feature_dim).astyp...]
  transfers between devices with their start and end apart: 3 -> 4, of which waited for: 2 -> 2; matrix products, arithmetic and copies ran while one was open for 14% -> 11% of each run, Pallas kernels for 0% -> 0%
where the time goes in v1:
time: 372 us; the launch traced here: 369 us
  blocking collectives  139 us (37%)
  waiting for transfers between devices  131 us (35%)
  other arithmetic  29.3 us (8%)
  matrix products  26.5 us (7%)
  local copies, waits for them, and re-layouts  21.6 us (6%)
  between operations  16.5 us (4%)
  starting transfers between devices  4.97 us (1%)
    psum x1, waiting for transfers between devices, on_device(): lax.psum((query_part, key_part, value_part, out_part, spd_part, degree_pa...  110 us
    psum x1, blocking collectives, on_device(): lax.psum((query_part, key_part, value_part, out_part, spd_part, degree_pa...  72.5 us
    all_to_all x1, blocking collectives, on_device(): lax.all_to_all(send_back.reshape(peer_count, capacity, feature_dim).astyp...  43.3 us
    all_to_all x1, waiting for transfers between devices, on_device(): lax.all_to_all(embed_table[safe_rows].reshape(peer_count, capacity, featu...  21.6 us
    all_to_all x1, blocking collectives, on_device(): lax.all_to_all(requests.reshape(peer_count, capacity), 'batch', split_axi...  20.9 us
  transfers between devices with their start and end apart: 4, of which 2 were waited for; matrix products, arithmetic and copies ran while one was open for 11% of the time, Pallas kernels for 0%

profile of v1, /device:TPU:8, one launch (start us, length us, event | category | flops | bytes accessed | tf_op | source)
XLA Modules:
  0.0 369.5 jit_solution(15018562542032013902)
XLA Ops:
  8.0 0.8 fusion.50
  8.8 0.6 reduce-window.6
  9.4 0.2 slice_reduce_fusion
  9.7 0.8 fusion.49
  10.4 0.7 compare_select_fusion.4
  11.1 1.6 scatter_custom_fusion
  12.8 20.9 %all_to_all.19 = s32[32,1,12]{2,1,0:T(1,128)S(1)} all-to-all(s32[32,1,12]{2,1,0:T(1,128)S(1)} %bitcast.120), channel_id=1, replica_groups=mesh['batch'=32,'node'=4,'replica'=2] {'batch'}, dimensions={0} | all-to-all | bytes 3072 | tf_op jit(solution)/shard_map/all_to_all | solution.py:48
  33.7 0.5 broadcast.245
  34.2 0.7 reduce.17
  35.0 0.6 fusion.53
  35.6 2.1 gather_fusion
  37.7 1.1 reshape.327
  38.9 4.7 %all-to-all-start.1 = ((bf16[32,12,1024]{2,1,0:T(8,128)(2,1)}), bf16[32,12,1024]{2,1,0:T(8,128)(2,1)}, u32[]{:S(2)}, u32[]{:S(2)}) async-start(bf16[32,12,1024]{2,1,0:T(8,128)(2,1)} %reshape.327), calls=%async_computation.1 | async-start | bytes 2097152 | tf_op jit(solution)/shard_map/all_to_all | solution.py:54
  43.6 1.3 fusion.2
  44.9 1.4 copy.39
  47.0 0.2 convolution_bitcast_fusion
  47.2 2.3 convolution_convert_fusion.3
  49.5 21.6 %all-to-all-done.1 = bf16[32,12,1024]{2,1,0:T(8,128)(2,1)} async-done(((bf16[32,12,1024]{2,1,0:T(8,128)(2,1)}), bf16[32,12,1024]{2,1,0:T(8,128)(2,1)}, u32[]{:S(2)}, u32[]{:S(2)}) %all-to-all-start.1) | async-done | bytes 786464 | tf_op jit(solution)/shard_map/all_to_all | solution.py:54
  71.1 1.3 reshape.328
  72.4 1.2 gather_fusion.1
  73.6 0.1 convert_reduce_fusion
  73.7 0.3 fusion.26
  74.0 1.5 convolution_convert_fusion.5
  75.5 0.5 convolution_convert_fusion.4
  76.0 0.4 fusion.11
  76.4 0.8 fusion.67
  77.2 0.5 convolution_convert_fusion.2
  77.7 0.4 multiply_reduce_fusion
  78.1 0.2 fusion.66
  78.3 0.2 fusion.17
  78.5 0.8 copy-done.1
  79.3 0.3 fusion.18
  79.6 2.1 convolution_convert_fusion.1
  81.7 2.8 convolution_convert_fusion
  84.5 1.4 fusion.60
  85.9 1.5 fusion.58
  87.4 1.4 fusion.56
  88.8 1.3 fusion.31
  90.2 0.2 reduce-scatter.4.cloned.1.call-start
  90.5 1.4 fusion.68
  91.9 1.4 convolution_add_fusion.1
  93.3 1.4 fusion.65
  94.8 3.8 %scatter_custom_fusion.1 = f32[384,1024]{1,0:T(8,128)} fusion(s32[256]{0:T(256)} %bitcast.125, bf16[256,1024]{1,0:T(8,128)(2,1)S(1)} %gather_fusion.1, f32[256,1024]{1,0:T(8,128)} %get-tuple-element.29, f32[]{:T(128)} %constant.15.clone.1, f32[256]{0:T(256)S(1)} %get-tuple-element.30, f32[256]{0:T(256)S(1)} %get-tuple-element.31, ...), kind=kCustom, calls=%fused_computation.44 | custom fusion | flops 2883584 | bytes 3674884 | tf_op jit(solution)/shard_map/scatter | solution.py:145
  98.5 2.4 convert_element_type.111
  100.9 1.2 convert_element_type.112
  102.2 43.3 %all_to_all.20 = bf16[32,12,1024]{2,1,0:T(8,128)(2,1)} all-to-all(bf16[32,12,1024]{2,1,0:T(8,128)(2,1)S(1)} %convert_element_type.112), channel_id=1, replica_groups=mesh['batch'=32,'node'=4,'replica'=2] {'batch'}, dimensions={0} | all-to-all | bytes 1572864 | tf_op jit(solution)/shard_map/all_to_all | solution.py:148
  145.5 2.4 reshape.377
  147.9 6.7 %scatter_custom_fusion.2 = f32[1024,1024]{1,0:T(8,128)} fusion(s32[384]{0:T(512)} %get-tuple-element.10, f32[384,1024]{1,0:T(8,128)} %reshape.377, f32[]{:T(128)} %constant.15.clone.1), kind=kCustom, calls=%fused_computation.11 | custom fusion | flops 393216 | bytes 4194816 | tf_op jit(solution)/shard_map/scatter-add | solution.py:159
  154.5 3.8 %convert_element_type.113 = bf16[1024,1024]{1,0:T(8,128)(2,1)} convert(f32[1024,1024]{1,0:T(8,128)} %scatter_custom_fusion.2) | non-fusion elementwise | flops 1048576 | bytes 6291456 | tf_op jit(solution)/shard_map/convert_element_type | solution.py:162
  158.4 4.0 %copy.52 = bf16[1024,1024]{0,1:T(8,128)(2,1)} copy(bf16[1024,1024]{1,0:T(8,128)(2,1)} %convert_element_type.113) | data formatting | bytes 4194304
  162.4 109.8 %all-reduce.7.cloned.1.call-done = (f32[1024,256]{1,0:T(8,128)}, f32[1024,256]{1,0:T(8,128)}, f32[1024,256]{1,0:T(8,128)}, f32[256,1024]{1,0:T(8,128)}) async-done(((f32[1024,256]{1,0:T(8,128)}, f32[1024,256]{1,0:T(8,128)}, f32[1024,256]{1,0:T(8,128)}, f32[256,1024]{1,0:T(8,128)}), (f32[1024,256]{1,0:T(8,128)}, f32[1024,256]{1,0:T(8,128)}, f32[1024,256]{1,0:T(8,128)}, ...) | async-done | bytes 4194320 | tf_op jit(solution)/shard_map/psum | solution.py:165
  272.3 1.2 copy-done.2
  273.5 1.3 copy.46
  274.8 3.9 %fusion.19 = f32[16,4]{0,1:T(4,128)S(1)} fusion(f32[4,256,256]{2,0,1:T(4,128)} %copy.46, s32[256,256]{1,0:T(8,128)S(1)} %bitcast.117), kind=kOutput, calls=%fused_computation.39 | convolution fusion | flops 51380224 | bytes 1310976 | tf_op jit(solution)/shard_map/gijb,ghij->bh/dot_general | solution.py:111
  278.7 0.2 fusion.44
  279.0 72.5 %all-reduce = (f32[16,4]{0,1:T(4,128)S(1)}, f32[32,4]{0,1:T(4,128)S(1)}) all-reduce(f32[16,4]{0,1:T(4,128)S(1)} %fusion.19, f32[32,4]{0,1:T(4,128)S(1)} %fusion.44), channel_id=1, replica_groups=mesh['batch'=32,'node'=4,'replica'=2] {'batch'}, use_global_device_ids=true, to_apply=%region_22.23 | all-reduce | flops 192 | bytes 1536 | tf_op jit(solution)/shard_map/psum | solution.py:165
  351.5 2.5 all-reduce.2
  353.9 0.6 broadcast_multiply_fusion.5
  354.5 0.6 broadcast_multiply_fusion.4
  355.1 1.1 copy.53
  356.2 0.8 convert_element_type.114
  357.1 2.4 broadcast_multiply_fusion.3
  359.5 1.1 broadcast_multiply_fusion
  360.6 1.5 broadcast_multiply_fusion.1
  (61 shorter events, 0.6 us)
Async XLA Ops:
  8.0 27.6 %copy-start = (bf16[1024,1024]{1,0:T(8,128)(2,1)S(1)}, bf16[1024,1024]{1,0:T(8,128)(2,1)}, u32[]{:S(2)}) copy-start(bf16[1024,1024]{1,0:T(8,128)(2,1)} %param.13) | copy-start | bytes 6291460
  11.1 35.8 %copy-start.15 = (s32[256,1]{0,1:T(1,128)}, s32[256,1]{0,1:T(1,128)S(1)}, u32[]{:S(2)}) copy-start(s32[256,1]{0,1:T(1,128)S(1)} %compare_select_fusion.4) | copy-start | bytes 3076
  37.7 5.9 %copy-start.12 = (s32[1,256,256]{2,1,0:T(8,128)S(1)}, s32[1,256,256]{2,1,0:T(8,128)}, u32[]{:S(2)}) copy-start(s32[1,256,256]{2,1,0:T(8,128)} %param.17) | copy-start | bytes 786436
  37.7 5.9 %copy-start.16 = (f32[16,4]{0,1:T(4,128)S(1)}, f32[16,4]{0,1:T(4,128)}, u32[]{:S(2)}) copy-start(f32[16,4]{0,1:T(4,128)} %param.23) | copy-start | bytes 772
  38.9 32.2 %all-to-all-start.1 = ((bf16[32,12,1024]{2,1,0:T(8,128)(2,1)}), bf16[32,12,1024]{2,1,0:T(8,128)(2,1)}, u32[]{:S(2)}, u32[]{:S(2)}) async-start(bf16[32,12,1024]{2,1,0:T(8,128)(2,1)} %reshape.327), calls=%async_computation.1 | async-start | bytes 2097152 | tf_op jit(solution)/shard_map/all_to_all | solution.py:54
  43.5 3.4 copy-start.17
  43.5 3.4 copy-start.18
  43.5 228.7 %all-reduce.7.cloned.1.call-start = ((), (), s32[]{:S(2)}) async-start(), calls=%async_computation.5 | async-start | bytes 8388608 | tf_op jit(solution)/shard_map/psum | solution.py:165
  73.6 2.0 copy-start.11
  73.6 2.4 copy-start.3
  76.0 1.2 copy-start.9
  76.4 1.6 copy-start.4
  76.4 1.3 copy-start.20
  77.7 0.7 copy-start.21
  78.3 1.0 copy-start.1
  79.6 2.1 copy-start.22
  85.9 2.9 copy-start.5
  85.9 2.9 copy-start.14
  90.2 264.9 %reduce-scatter.4.cloned.1.call-start = ((), (), s32[]{:S(2)}) async-start(), calls=%async_computation.4 | async-start | bytes 2359296
  90.5 2.9 copy-start.10
  162.4 194.7 %all-reduce.9.cloned.1.call-start = ((), (), s32[]{:S(2)}) async-start(), calls=%async_computation.6 | async-start | bytes 8388608 | tf_op jit(solution)/shard_map/psum | solution.py:164
  272.2 1.2 copy-start.2
  273.5 1.3 copy-start.13
  273.5 5.3 %copy-start.19 = (s32[1,256]{1,0:T(1,128)S(1)}, s32[1,256]{1,0:T(1,128)}, u32[]{:S(2)}) copy-start(s32[1,256]{1,0:T(1,128)} %param.18) | copy-start | bytes 3076
  357.1 2.4 copy-start.6
  357.1 3.5 copy-start.7
  357.1 3.5 copy-start.8
Sparse Core Ops, SparseCore 0:
  90.3 181.8 all-reduce.6
  275.5 36.7 all-reduce.8
Sparse Core Ops, SparseCore 1:
  162.4 31.5 reduce-scatter.3
